TPU v7x, 512 devices: a whole 4x8x8 slice. The times are simulated.
512 devices in a mesh: gx: 8 (over z), gy: 8 (over y), gz: 8 (over x, core).
Axes of the slice: x: 4, y: 8, z: 8, core: 2. Of those that a mesh axis runs over, the one named last changes fastest.
Arguments:
- hidden_states: bfloat16 [512, 8192], P(('gx', 'gy'), 'gz'), may hold values from -17 to 17
- weight: bfloat16 [8192, 65536], P('gz', ('gx', 'gy')), may hold values from -1 to 1
- targets: int32 [512], replicated, may hold values from 0 to 65535
- upstream: bfloat16 [512], replicated, may hold values from 8 to 64
Outputs:
- grad_hidden: bfloat16 [512, 8192], P(('gx', 'gy'), 'gz')
- grad_weight: bfloat16 [8192, 65536], P('gz', ('gx', 'gy'))
All inputs are finite; a program needn't handle non-finite values.
Results may differ from a plain program's by a relative error of at most 0.009.
Values may be sent and summed in bfloat16 or wider, within the bound.
A program may use at most 64 MiB of HBM per device.

v0:
```python
import jax
import jax.numpy as jnp
from jax import lax
from jax.sharding import PartitionSpec as P


def softmax_grad(logits, chosen, scaling, columns):
    local_max = jnp.max(logits, axis=1)
    local_exp = jnp.exp(logits - local_max[:, None])
    row_peak = lax.pmax(local_max, ("gx", "gy"))
    local_sum = jnp.sum(local_exp, axis=1) * jnp.exp(local_max - row_peak)
    row_sum = lax.psum(local_sum, ("gx", "gy"))
    factor = jnp.exp(local_max - row_peak) / row_sum
    probability = local_exp * factor[:, None]
    one_hot = (chosen[:, None] == columns[None, :]).astype(jnp.float32)
    return (scaling.astype(jnp.float32)[:, None] * (probability - one_hot)).astype(jnp.bfloat16)


def body(hidden_states, weight, targets, upstream):
    gathered = lax.all_gather(hidden_states, ("gx", "gy"), axis=0, tiled=True)
    partial_value = jnp.dot(gathered, weight, preferred_element_type=jnp.float32)
    block_width = weight.shape[1]
    vocab_block = lax.axis_index(("gx", "gy"))
    columns = vocab_block * block_width + jnp.arange(block_width, dtype=jnp.int32)
    summed = lax.psum(partial_value, "gz")
    grad_logits = softmax_grad(summed, targets, upstream, columns)
    grad_weight = lax.dot_general(
        gathered, grad_logits, (((0,), (0,)), ((), ())), preferred_element_type=jnp.float32
    ).astype(jnp.bfloat16)
    grad_hidden = lax.psum_scatter(
        lax.dot_general(
            grad_logits, weight, (((1,), (1,)), ((), ())), preferred_element_type=jnp.float32
        ),
        ("gx", "gy"),
        scatter_dimension=0,
        tiled=True,
    ).astype(jnp.bfloat16)
    return (grad_hidden, grad_weight)


def solution(mesh):
    placed = (P(("gx", "gy"), "gz"), P("gz", ("gx", "gy")), P(), P())
    return jax.shard_map(
        body,
        mesh=mesh,
        in_specs=placed,
        out_specs=(P(("gx", "gy"), "gz"), P("gz", ("gx", "gy"))),
        check_vma=False,
    )
```

profile of v0, /device:TPU:6, one launch (start us, length us, event | category | flops | bytes accessed | tf_op | source)
XLA Modules:
  0.0 778.1 jit_solution(10867516294637219455)
XLA Ops:
  7.2 0.0 copy-start
  7.2 0.0 all-gather.2.cloned.1.call-start
  7.2 0.7 all-gather.2.cloned.1.call-update
  7.9 0.0 all-reduce.4.cloned.1.call-start
  8.0 89.6 %all-gather.2.cloned.1.call-done = bf16[512,1024]{1,0:T(8,128)(2,1)} async-done(((bf16[8,1024]{1,0:T(8,128)(2,1)}), bf16[512,1024]{1,0:T(8,128)(2,1)}) %all-gather.2.cloned.1.call-update) | async-done | bytes 1048592 | tf_op jit(solution)/shard_map/all_gather | solution.py:20
  97.5 0.0 copy-done
  97.5 3.8 fusion.3
  101.3 0.0 copy-start.3
  101.3 0.0 all-reduce.4.cloned.1.call-update
  101.4 0.6 copy-done.3
  102.0 1.3 dynamic-slice
  104.0 0.0 copy-start.2
  104.0 68.5 %all-reduce.4.cloned.1.call-done = f32[512,1024]{1,0:T(8,128)} async-done(((f32[512,1024]{1,0:T(8,128)}), f32[512,1024]{1,0:T(8,128)}) %all-reduce.4.cloned.1.call-update) | async-done | bytes 2097168 | tf_op jit(solution)/shard_map/psum | solution.py:25
  172.5 1.8 reduce_max.9
  174.2 144.2 %pmax.7 = f32[512]{0:T(512)S(1)} all-reduce(f32[512]{0:T(512)S(1)} %reduce_max.9), channel_id=1, replica_groups=mesh['gx'=8,'gy'=8,'gz'=8] {'gx','gy'}, use_global_device_ids=true, to_apply=%region_2.0 | all-reduce | flops 512 | bytes 4096 | tf_op jit(solution)/shard_map/pmax | solution.py:10
  318.4 2.0 fusion
  320.5 138.0 %psum.15 = f32[512]{0:T(512)S(1)} all-reduce(f32[512]{0:T(512)S(1)} %fusion.2), channel_id=1, replica_groups=mesh['gx'=8,'gy'=8,'gz'=8] {'gx','gy'}, use_global_device_ids=true, to_apply=%region_4.0 | all-reduce | flops 512 | bytes 4096 | tf_op jit(solution)/shard_map/psum | solution.py:12
  458.4 0.0 copy-done.2
  458.4 2.2 multiply_convert_fusion
  460.7 0.0 copy-start.1
  460.7 1.0 copy-done.1
  461.7 2.6 fusion.4
  464.3 298.2 %all-reduce.5 = bf16[512,1024]{1,0:T(8,128)(2,1)S(1)} all-reduce(f32[512,1024]{1,0:T(8,128)} %fusion.4), channel_id=2, replica_groups=mesh['gx'=8,'gy'=8,'gz'=8] {'gx','gy'}, use_global_device_ids=true, to_apply=%region_5.0.clone | all-reduce | flops 524288 | bytes 3145728
  762.5 4.2 convert_bitcast_fusion
  766.7 3.9 copy.7
  770.6 0.6 dynamic-slice_convert_fusion
  (4 shorter events, 0.0 us)
Async XLA Ops:
  7.2 90.4 %copy-start = (bf16[1024,1024]{1,0:T(8,128)(2,1)S(1)}, bf16[1024,1024]{1,0:T(8,128)(2,1)}, u32[]{:S(2)}) copy-start(bf16[1024,1024]{1,0:T(8,128)(2,1)} %param.5) | copy-start | bytes 6291460
  7.2 90.4 %all-gather.2.cloned.1.call-start = ((), (), s32[]{:S(2)}) async-start(), calls=%async_computation | async-start | bytes 1064960 | tf_op jit(solution)/shard_map/all_gather | solution.py:20
  7.9 164.5 %all-reduce.4.cloned.1.call-start = ((), (), s32[]{:S(2)}) async-start(), calls=%async_computation.1 | async-start | bytes 4194304 | tf_op jit(solution)/shard_map/psum | solution.py:25
  101.3 0.7 copy-start.3
  104.0 354.5 %copy-start.2 = (s32[512]{0:T(512)S(1)}, s32[512]{0:T(512)}, u32[]{:S(2)}) copy-start(s32[512]{0:T(512)} %param.6) | copy-start | bytes 6148
  460.7 1.0 copy-start.1
Sparse Core Ops, SparseCore 0:
  11.1 86.4 all-gather.1
  101.5 70.9 all-reduce.3
where the time goes:
time: 779 us; the launch traced here: 778 us
  blocking collectives  580 us (74%)
  waiting for transfers between devices  159 us (20%)
  between operations  14.8 us (2%)
  matrix products  10.6 us (1%)
    unnamed x1, blocking collectives  298 us
    pmax x1, blocking collectives, softmax_grad(): row_peak = lax.pmax(local_max, ('gx', 'gy'))  144 us
    psum x1, blocking collectives, softmax_grad(): row_sum = lax.psum(local_sum, ('gx', 'gy'))  138 us
    all_gather x1, waiting for transfers between devices, body(): gathered = lax.all_gather(hidden_states, ('gx', 'gy'), axis=0, tiled=True)  89.6 us
    psum x1, waiting for transfers between devices, body(): summed = lax.psum(partial_value, 'gz')  68.5 us
  transfers between devices with their start and end apart: 2, of which 2 were waited for; matrix products, arithmetic and copies ran while one was open for 0% of the time, Pallas kernels for 0%

commit v1 on v0

v1 whole, which is shorter than its diff:
```python
import functools

import jax
import jax.numpy as jnp
from jax import lax
from jax.experimental import pallas as pl
from jax.experimental.pallas import tpu as pltpu
from jax.sharding import PartitionSpec as P

MESH = pl.DeviceIdType.MESH
F32, BF16, I32 = jnp.float32, jnp.bfloat16, jnp.int32
FAR_FIRST = (4, 3, 5, 2, 6, 1, 7)
GROUP = ((2, 0), (2, 1), (1, 0), (3, 0), (1, 1), (3, 1), (0, 1))


def remote(src, dst, send_sem, recv_sem, device):
    return pltpu.make_async_remote_copy(
        src_ref=src, dst_ref=dst, send_sem=send_sem, recv_sem=recv_sem, device_id=device, device_id_type=MESH
    )


def upper_rows(shape):
    return lax.broadcasted_iota(I32, shape, 0) < 4


def pack(a):
    q = [a[:, 256 * k : 256 * (k + 1)] for k in range(4)]
    t = [pltpu.roll(x, 4, 0) for x in q]
    first = upper_rows((8, 256))
    low = jnp.concatenate([jnp.where(first, q[0], t[1]), jnp.where(first, q[2], t[3])], axis=0)
    high = jnp.concatenate([jnp.where(first, t[0], q[1]), jnp.where(first, t[2], q[3])], axis=0)
    return low, high


def unpack(low, high):
    first = upper_rows((8, 256))
    parts = []
    for k in range(2):
        a, c = low[8 * k : 8 * k + 8], high[8 * k : 8 * k + 8]
        parts.append(jnp.where(first, a, pltpu.roll(c, 4, 0)))
        parts.append(jnp.where(first, pltpu.roll(a, 4, 0), c))
    return jnp.concatenate(parts, axis=1)


def rows_of(*rows):
    sub = lax.broadcasted_iota(I32, (8, 128), 0)
    out = jnp.zeros((8, 128), F32)
    for k, row in enumerate(rows):
        out = jnp.where(sub == k, jnp.broadcast_to(row, (8, 128)), out)
    return out


def combine(stats):
    peaks = [stats[k, 0:1, :] for k in range(stats.shape[0])]
    peak = functools.reduce(jnp.maximum, peaks)
    scale = [jnp.exp(p - peak) for p in peaks]
    total = sum(stats[k, 1:2, :] * scale[k] for k in range(stats.shape[0]))
    chosen = sum(stats[k, 2:3, :] * scale[k] for k in range(stats.shape[0]))
    return peak, total, chosen


def kernel(
    h_ref, w_hbm, tgt_ref, up_ref, gh_ref, gw_hbm,
    w, hid, a1s, a1r, keep, cs, cr, xs, xr, e_all, g, p, r1, s2, r2, gwv,
    own_col, stat_col, st_a, st_b, st_c, t_col,
    w_sem, gw_sem, a1_ss, a1_rs, a2_ss, a2_rs, c_ss, c_rs, x_ss, x_rs,
    e_ss, e_rs, sa_ss, sa_rs, sb_ss, sb_rs, sc_ss, sc_rs, d1_ss, d1_rs, d2_ss, d2_rs,
):
    z, y, gz = lax.axis_index("gx"), lax.axis_index("gy"), lax.axis_index("gz")
    xx, core = gz // 2, gz % 2
    vocab = w.shape[1]
    zp, yp = z // 2, y // 2
    me = (z, y)

    def along(kind, d):
        return (z, (y + d) % 8, gz) if kind == 0 else ((z + d) % 8, y, gz)

    def member(dx, flip):
        c = 1 - core if flip else core
        return ((xx + dx) % 4) * 2 + c

    load_w = pltpu.make_async_copy(w_hbm, w, w_sem)
    load_w.start()

    barrier = pltpu.get_barrier_semaphore()
    for d in FAR_FIRST:
        for kind in (0, 1):
            pl.semaphore_signal(barrier, inc=1, device_id=along(kind, d), device_id_type=MESH)
    for dx, flip in GROUP:
        pl.semaphore_signal(barrier, inc=1, device_id=(z, y, member(dx, flip)), device_id_type=MESH)

    low, high = pack(h_ref[...].astype(F32))
    a1s[0] = low.astype(BF16)
    a1s[1] = high.astype(BF16)
    a1r[0, y] = low.astype(BF16)
    a1r[1, z] = high.astype(BF16)

    k = lax.broadcasted_iota(I32, (128, 512), 0)
    t = lax.broadcasted_iota(I32, (128, 512), 1)
    block = 2 * (k >> 4) + xx // 2
    other = (xx % 2) * 4 + ((k >> 2) & 3)
    zt = jnp.where(core == 0, block, other)
    yt = jnp.where(core == 0, other, block)
    token = zt * 64 + yt * 8 + core * 4 + (k & 3)
    select = jnp.where((token == t) & (k < 64), 1.0, 0.0).astype(BF16)
    tgt = tgt_ref[...]
    sub = lax.broadcasted_iota(I32, (128, 512), 0)
    values = jnp.where(sub == 0, jnp.broadcast_to((tgt >> 8).astype(F32), (128, 512)), 0.0)
    values = jnp.where(sub == 1, jnp.broadcast_to((tgt & 255).astype(F32), (128, 512)), values)
    values = jnp.where(sub == 2, jnp.broadcast_to(up_ref[...].astype(F32), (128, 512)), values).astype(BF16)
    contract = (((1,), (1,)), ((), ()))
    own_col[...] = lax.dot_general(select, values, contract, preferred_element_type=F32)
    own_row = lax.dot_general(values, select, contract, preferred_element_type=F32)
    tgt_row = own_row[0:1, :] * 256.0 + own_row[1:2, :]
    up_row = own_row[2:3, :]
    stat_col[...] = jnp.zeros((128, 128), F32)

    pl.semaphore_wait(barrier, 21)

    sends = []
    for d in FAR_FIRST:
        for kind in (0, 1):
            c = remote(a1s.at[kind], a1r.at[kind, me[1 - kind]], a1_ss.at[kind, d], a1_rs.at[kind, me[1 - kind]], along(kind, d))
            c.start()
            sends.append(c)

    def arrived(dst, sem, peer):
        remote(dst, dst, w_sem, sem, peer).wait_recv()

    for kind in (0, 1):
        mine = me[1 - kind]
        for d in range(1, 8):
            src = (mine + d) % 8
            arrived(a1r.at[kind, src], a1_rs.at[kind, src], along(kind, 1))
        for b in range(2):
            rows = [
                unpack(a1r[kind, 4 * b + 2 * q].astype(F32), a1r[kind, 4 * b + 2 * q + 1].astype(F32)) for q in range(2)
            ]
            hid[kind, me[kind], 16 * b : 16 * b + 16, :] = jnp.concatenate(rows, axis=0).astype(BF16)
        for d in (1, 7, 2, 6, 3, 5, 4):
            slot = hid.at[kind, me[kind]]
            c = remote(slot, slot, a2_ss.at[kind, d], a2_rs.at[kind, me[kind]], along(1 - kind, d))
            c.start()
            sends.append(c)

    load_w.wait()

    def shift(s, parity):
        return (0, 2 * parity + 3, 5 - 2 * parity, 2)[s]

    def pair_of(kind, s):
        return (zp + shift(s, z % 2)) % 4 if kind == 0 else (yp + shift(s, y % 2)) % 4

    def own_pair(s):
        return jnp.where(core == 0, pair_of(0, s), pair_of(1, s))

    def other_pair(s):
        return jnp.where(core == 0, pair_of(1, s), pair_of(0, s))

    sibling = (z, y, member(0, 1))

    def multiply(s):
        for kind in (0, 1):
            pair = pair_of(kind, s)
            if s == 0:
                chunks = [4 * pair + 1 - me[kind]]
            else:
                chunks = [2 * pair, 2 * pair + 1]
            for q in chunks:
                arrived(hid.at[kind, q], a2_rs.at[kind, q], along(1 - kind, 1))
        mine, others = own_pair(s), other_pair(s)

        def tile(n, _):
            lanes = pl.ds(pl.multiple_of(n * 256, 256), 256)
            lhs = jnp.concatenate(
                [hid[core, pl.ds(2 * mine, 2)].reshape(64, 1024), hid[1 - core, pl.ds(2 * others, 2)].reshape(64, 1024)],
                axis=0,
            )
            part = jnp.dot(lhs, w[:, lanes], preferred_element_type=F32)
            keep[s, :, lanes] = part[:64]
            cs[s, :, lanes] = part[64:]
            return 0

        lax.fori_loop(0, 4, tile, 0)
        c = remote(cs.at[s], cr.at[s], c_ss.at[s], c_rs.at[s], sibling)
        c.start()
        sends.append(c)

    def pass_on(s):
        arrived(cr.at[s], c_rs.at[s], sibling)
        xs[s] = keep[s] + cr[s]
        for dx in (2, 1, 3):
            to = (xx + dx) % 4
            c = remote(
                xs.at[s, pl.ds(pl.multiple_of(to * 16, 16), 16)], xr.at[s, dx - 1], x_ss.at[s, dx - 1], x_rs.at[s, dx - 1],
                (z, y, member(dx, 0)),
            )
            c.start()
            sends.append(c)

    def finish(s):
        for dx in (2, 1, 3):
            arrived(xr.at[s, dx - 1], x_rs.at[s, dx - 1], sibling)
        pair = own_pair(s)
        logits = xs[s, pl.ds(pl.multiple_of(xx * 16, 16), 16), :] + xr[s, 0] + xr[s, 1] + xr[s, 2]
        rows = pl.ds(pl.multiple_of(pair * 16, 16), 16)
        info = own_col[rows, :]
        target = info[:, 0:1] * 256.0 + info[:, 1:2]
        column = lax.broadcasted_iota(I32, (16, vocab), 1) + (z * 8 + y) * vocab
        hit = column.astype(F32) == target
        peak = jnp.max(logits, axis=1, keepdims=True)
        value = jnp.exp(logits - peak)
        rest = jnp.where(hit, 0.0, value)
        e_all[gz, pair] = rest.astype(BF16)
        for i, (dx, flip) in enumerate(GROUP):
            slot = e_all.at[gz, pair]
            remote(slot, slot, e_ss.at[i], e_rs.at[gz], (z, y, member(dx, flip))).start()
        total = jnp.sum(rest, axis=1, keepdims=True)
        chosen = jnp.sum(jnp.where(hit, value, 0.0), axis=1, keepdims=True)
        lane = lax.broadcasted_iota(I32, (16, 128), 1)
        stat_col[rows, :] = jnp.where(lane == 0, peak, jnp.where(lane == 1, total, jnp.where(lane == 2, chosen, 0.0)))

    for s in range(6):
        if s < 4:
            multiply(s)
        if 1 <= s < 5:
            pass_on(s - 1)
        if s >= 2:
            finish(s - 2)

    def exchange(buf, ss, rs, kind):
        for d in FAR_FIRST:
            c = remote(buf.at[0], buf.at[d], ss.at[d], rs.at[d], along(kind, d))
            c.start()
            sends.append(c)
        for d in FAR_FIRST:
            arrived(buf.at[d], rs.at[d], along(kind, d))
        return combine(buf[...])

    mine = stat_col[...].T[0:8, :]
    st_a[0] = mine
    peak, total, chosen = exchange(st_a, sa_ss, sa_rs, 0)
    st_b[0] = rows_of(peak, total, chosen)
    peak, total, chosen = exchange(st_b, sb_ss, sb_rs, 1)
    used = lax.broadcasted_iota(I32, (1, 128), 1) < 64
    scale = up_row / jnp.where(used, total + chosen, 1.0)
    st_c[gz] = rows_of(scale * jnp.exp(mine[0:1, :] - peak), -scale * total, tgt_row)
    for i, (dx, flip) in enumerate(GROUP):
        c = remote(st_c.at[gz], st_c.at[gz], sc_ss.at[i], sc_rs.at[gz], (z, y, member(dx, flip)))
        c.start()
        sends.append(c)
    for i, (dx, flip) in enumerate(GROUP):
        j = member(dx, flip)
        arrived(e_all.at[j], e_rs.at[j], sibling)
    for i, (dx, flip) in enumerate(GROUP):
        j = member(dx, flip)
        arrived(st_c.at[j], sc_rs.at[j], sibling)
    t_col[...] = jnp.concatenate([st_c[...].reshape(64, 128), jnp.zeros((64, 128), F32)], axis=0).T

    def logit_grads(kind, pair):
        column = (lax.broadcasted_iota(I32, (16, vocab), 1) + (z * 8 + y) * vocab).astype(F32)
        info = t_col[pl.ds(pl.multiple_of(pair * 16, 16), 16), :]
        for x in range(4):
            j = 2 * x + kind
            value = info[:, 8 * j : 8 * j + 1] * e_all[j, pair].astype(F32)
            value = jnp.where(column == info[:, 8 * j + 2 : 8 * j + 3], info[:, 8 * j + 1 : 8 * j + 2], value)
            g[kind, 2 * pair + x // 2, 16 * (x % 2) : 16 * (x % 2) + 16, :] = value.astype(BF16)

    for step, change in enumerate((2, 1, 3, 0)):
        pairs = ((zp + change) % 4, (yp + change) % 4)
        for kind in (0, 1):
            logit_grads(kind, pairs[kind])

        def tile(n, _):
            lanes = pl.ds(pl.multiple_of(n * 256, 256), 256)
            lhs = jnp.concatenate([g[kind, pl.ds(2 * pairs[kind], 2)].reshape(64, vocab) for kind in (0, 1)], axis=0)
            part = lax.dot_general(lhs, w[lanes, :], contract, preferred_element_type=F32).astype(BF16)
            for kind in (0, 1):
                p[kind, pl.ds(2 * pairs[kind], 2), :, lanes] = part[64 * kind : 64 * kind + 64].reshape(2, 32, 256)
            return 0

        lax.fori_loop(0, 4, tile, 0)
        for kind in (0, 1):
            if change == 0:
                chunks = [4 * pairs[kind] + 1 - me[kind]]
                r1[kind, me[kind]] = p[kind, me[kind]]
            else:
                chunks = [2 * pairs[kind], 2 * pairs[kind] + 1]
            for i, q in enumerate(chunks):
                to = (q, y, gz) if kind == 0 else (z, q, gz)
                c = remote(p.at[kind, q], r1.at[kind, me[kind]], d1_ss.at[kind, 2 * step + i], d1_rs.at[kind, me[kind]], to)
                c.start()
                sends.append(c)

    def weight_tile(n, _):
        lanes = pl.ds(pl.multiple_of(n * 256, 256), 256)
        part = lax.dot_general(
            hid[:, :, :, lanes].reshape(512, 256), g[...].reshape(512, vocab), (((0,), (0,)), ((), ())),
            preferred_element_type=F32,
        )
        gwv[lanes, :] = part.astype(BF16)
        return 0

    lax.fori_loop(0, 4, weight_tile, 0)
    store_gw = pltpu.make_async_copy(gwv, gw_hbm, gw_sem)
    store_gw.start()

    for kind in (0, 1):
        for d in range(1, 8):
            src = (me[kind] + d) % 8
            arrived(r1.at[kind, src], d1_rs.at[kind, src], along(1 - kind, 1))
        for b in range(2):
            rows = sum(r1[kind, src, 16 * b : 16 * b + 16, :].astype(F32) for src in range(8))
            for q in range(2):
                low, high = pack(rows[8 * q : 8 * q + 8])
                s2[kind, 4 * b + 2 * q] = low.astype(BF16)
                s2[kind, 4 * b + 2 * q + 1] = high.astype(BF16)
        for d in FAR_FIRST:
            to = (me[1 - kind] + d) % 8
            c = remote(s2.at[kind, to], r2.at[kind, d], d2_ss.at[kind, d], d2_rs.at[kind, d], along(kind, d))
            c.start()
            sends.append(c)
    halves = []
    for kind in (0, 1):
        for d in FAR_FIRST:
            arrived(r2.at[kind, d], d2_rs.at[kind, d], along(kind, 1))
        halves.append(s2[kind, me[1 - kind]].astype(F32) + sum(r2[kind, d].astype(F32) for d in range(1, 8)))
    gh_ref[...] = unpack(*halves).astype(BF16)

    for c in sends:
        c.wait_send()
    for i, (dx, flip) in enumerate(GROUP):
        remote(e_all.at[gz], e_all.at[gz], e_ss.at[i], e_rs.at[gz], sibling).wait_send()
    store_gw.wait()


def body(hidden_states, weight, targets, upstream):
    vmem = pl.BlockSpec(memory_space=pltpu.VMEM)
    hbm = pl.BlockSpec(memory_space=pl.ANY)
    dma = pltpu.SemaphoreType.DMA
    scratch = [
        pltpu.VMEM((1024, 1024), BF16),
        pltpu.VMEM((2, 8, 32, 1024), BF16),
        pltpu.VMEM((2, 16, 256), BF16),
        pltpu.VMEM((2, 8, 16, 256), BF16),
        pltpu.VMEM((4, 64, 1024), F32),
        pltpu.VMEM((4, 64, 1024), F32),
        pltpu.VMEM((4, 64, 1024), F32),
        pltpu.VMEM((4, 64, 1024), F32),
        pltpu.VMEM((4, 3, 16, 1024), F32),
        pltpu.VMEM((8, 4, 16, 1024), BF16),
        pltpu.VMEM((2, 8, 32, 1024), BF16),
        pltpu.VMEM((2, 8, 32, 1024), BF16),
        pltpu.VMEM((2, 8, 32, 1024), BF16),
        pltpu.VMEM((2, 8, 16, 256), BF16),
        pltpu.VMEM((2, 8, 16, 256), BF16),
        pltpu.VMEM((1024, 1024), BF16),
        pltpu.VMEM((128, 128), F32),
        pltpu.VMEM((128, 128), F32),
        pltpu.VMEM((8, 8, 128), F32),
        pltpu.VMEM((8, 8, 128), F32),
        pltpu.VMEM((8, 8, 128), F32),
        pltpu.VMEM((128, 128), F32),
        dma, dma,
        dma((2, 8)), dma((2, 8)), dma((2, 8)), dma((2, 8)),
        dma((4,)), dma((4,)), dma((4, 3)), dma((4, 3)),
        dma((7,)), dma((8,)),
        dma((8,)), dma((8,)), dma((8,)), dma((8,)), dma((7,)), dma((8,)),
        dma((2, 8)), dma((2, 8)), dma((2, 8)), dma((2, 8)),
    ]
    return pl.pallas_call(
        kernel,
        out_shape=(
            jax.ShapeDtypeStruct(hidden_states.shape, BF16),
            jax.ShapeDtypeStruct(weight.shape, BF16),
        ),
        in_specs=[vmem, hbm, vmem, vmem],
        out_specs=(vmem, hbm),
        scratch_shapes=scratch,
        name="projection_backward",
        cost_estimate=pl.CostEstimate(flops=3 * 2 * 512 * 1024 * 1024, bytes_accessed=5 << 20, transcendentals=1 << 16),
        compiler_params=pltpu.CompilerParams(collective_id=0, has_side_effects=True, vmem_limit_bytes=48 << 20),
    )(hidden_states, weight, targets.reshape(1, 512), upstream.reshape(1, 512))


def solution(mesh):
    return jax.shard_map(
        body,
        mesh=mesh,
        in_specs=(P(("gx", "gy"), "gz"), P("gz", ("gx", "gy")), P(), P()),
        out_specs=(P(("gx", "gy"), "gz"), P("gz", ("gx", "gy"))),
        check_vma=False,
    )
```

time: 779 us -> 92 us (0.12)
  the two profiles are of different devices: /device:TPU:6 before, /device:TPU:1 now
where the time goes in v1:
time: 92 us; the launch traced here: 91.2 us
  Pallas kernels  85 us (92%)
  local copies, waits for them, and re-layouts  5.6 us (6%)
    pallas_call x1, Pallas kernels, body(): pl.pallas_call(kernel, out_shape=(jax.ShapeDtypeStruct(hidden_states.shap...  85 us
    unnamed x8, local copies, waits for them, and re-layouts  4.91 us

profile of v1, /device:TPU:1, one launch (start us, length us, event | category | flops | bytes accessed | tf_op | source)
XLA Modules:
  0.0 91.2 jit_solution(6940901745370790204)
XLA Ops:
  0.6 0.7 reshape.11.up_ref
  1.3 0.0 copy-start
  1.3 1.6 %copy-done = bf16[1024,1024]{1,0:T(8,128)(2,1)S(1)} copy-done((bf16[1024,1024]{1,0:T(8,128)(2,1)S(1)}, bf16[1024,1024]{1,0:T(8,128)(2,1)}, u32[]{:S(2)}) %copy-start) | copy-done | bytes 2097176
  2.9 0.0 copy-start.1
  2.9 0.7 copy-done.1
  3.6 0.0 copy-start.2
  3.6 0.7 copy-done.2
  4.3 85.0 %projection_backward.1 = (bf16[8,1024]{1,0:T(8,128)(2,1)S(1)}, bf16[1024,1024]{1,0:T(8,128)(2,1)S(1)}) custom-call(bf16[8,1024]{1,0:T(8,128)(2,1)S(1)} %copy-done.1, bf16[1024,1024]{1,0:T(8,128)(2,1)S(1)} %copy-done, s32[1,512]{1,0:T(1,128)S(1)} %bitcast.1, bf16[1,512]{1,0:T(2,128)(2,1)S(1)} %reshape.11.up_ref), custom_call_target="tpu_custom_call" | custom-call | flops 3221225472 | bytes 5242880 | tf_op jit(solution)/shard_map/projection_backward/pallas_call | solution.py:371
  89.3 0.6 copy.8
  89.9 1.3 %copy.9 = bf16[1024,1024]{1,0:T(8,128)(2,1)} copy(bf16[1024,1024]{1,0:T(8,128)(2,1)S(1)} %get-tuple-element.5) | data formatting | bytes 4194304
Async XLA Ops:
  1.3 1.6 %copy-start = (bf16[1024,1024]{1,0:T(8,128)(2,1)S(1)}, bf16[1024,1024]{1,0:T(8,128)(2,1)}, u32[]{:S(2)}) copy-start(bf16[1024,1024]{1,0:T(8,128)(2,1)} %w_hbm.1) | copy-start | bytes 6291460
  2.9 0.7 copy-start.1
  3.6 0.7 copy-start.2

commit v2 on v1

--- a/solution.py
+++ b/solution.py
@@ -60,10 +60,10 @@
 
 
 def kernel(
-    h_ref, w_hbm, tgt_ref, up_ref, gh_ref, gw_hbm,
-    w, hid, a1s, a1r, keep, cs, cr, xs, xr, e_all, g, p, r1, s2, r2, gwv,
+    h_hbm, w_hbm, tgt_hbm, up_hbm, gh_ref, gw_ref,
+    w, wt, h_ref, tgt_ref, up_ref, hid, a1s, a1r, keep, cs, cr, xs, xr, e_all, g, p, r1, s2, r2,
     own_col, stat_col, st_a, st_b, st_c, t_col,
-    w_sem, gw_sem, a1_ss, a1_rs, a2_ss, a2_rs, c_ss, c_rs, x_ss, x_rs,
+    w_sem, in_sem, a1_ss, a1_rs, a2_ss, a2_rs, c_ss, c_rs, x_ss, x_rs,
     e_ss, e_rs, sa_ss, sa_rs, sb_ss, sb_rs, sc_ss, sc_rs, d1_ss, d1_rs, d2_ss, d2_rs,
 ):
     z, y, gz = lax.axis_index("gx"), lax.axis_index("gy"), lax.axis_index("gz")
@@ -81,6 +81,12 @@
 
     load_w = pltpu.make_async_copy(w_hbm, w, w_sem)
     load_w.start()
+    loads = [
+        pltpu.make_async_copy(src, dst, in_sem.at[i])
+        for i, (src, dst) in enumerate(((h_hbm, h_ref), (tgt_hbm, tgt_ref), (up_hbm, up_ref)))
+    ]
+    for c in loads:
+        c.start()
 
     barrier = pltpu.get_barrier_semaphore()
     for d in FAR_FIRST:
@@ -89,6 +95,8 @@
     for dx, flip in GROUP:
         pl.semaphore_signal(barrier, inc=1, device_id=(z, y, member(dx, flip)), device_id_type=MESH)
 
+    for c in loads:
+        c.wait()
     low, high = pack(h_ref[...].astype(F32))
     a1s[0] = low.astype(BF16)
     a1s[1] = high.astype(BF16)
@@ -107,13 +115,21 @@
     sub = lax.broadcasted_iota(I32, (128, 512), 0)
     values = jnp.where(sub == 0, jnp.broadcast_to((tgt >> 8).astype(F32), (128, 512)), 0.0)
     values = jnp.where(sub == 1, jnp.broadcast_to((tgt & 255).astype(F32), (128, 512)), values)
-    values = jnp.where(sub == 2, jnp.broadcast_to(up_ref[...].astype(F32), (128, 512)), values).astype(BF16)
+    values = jnp.where(sub == 2, jnp.broadcast_to(up_ref[...].reshape(1, 512).astype(F32), (128, 512)), values).astype(BF16)
     contract = (((1,), (1,)), ((), ()))
     own_col[...] = lax.dot_general(select, values, contract, preferred_element_type=F32)
     own_row = lax.dot_general(values, select, contract, preferred_element_type=F32)
     tgt_row = own_row[0:1, :] * 256.0 + own_row[1:2, :]
     up_row = own_row[2:3, :]
     stat_col[...] = jnp.zeros((128, 128), F32)
+    load_w.wait()
+
+    def turn(n, _):
+        lanes = pl.ds(pl.multiple_of(n * 256, 256), 256)
+        wt[:, lanes] = w[lanes, :].T
+        return 0
+
+    lax.fori_loop(0, 4, turn, 0)
 
     pl.semaphore_wait(barrier, 21)
 
@@ -125,7 +141,7 @@
             sends.append(c)
 
     def arrived(dst, sem, peer):
-        remote(dst, dst, w_sem, sem, peer).wait_recv()
+        remote(dst, dst, sem, sem, peer).wait_recv()
 
     for kind in (0, 1):
         mine = me[1 - kind]
@@ -143,8 +159,6 @@
             c.start()
             sends.append(c)
 
-    load_w.wait()
-
     def shift(s, parity):
         return (0, 2 * parity + 3, 5 - 2 * parity, 2)[s]
 
@@ -170,18 +184,12 @@
                 arrived(hid.at[kind, q], a2_rs.at[kind, q], along(1 - kind, 1))
         mine, others = own_pair(s), other_pair(s)
 
-        def tile(n, _):
-            lanes = pl.ds(pl.multiple_of(n * 256, 256), 256)
-            lhs = jnp.concatenate(
-                [hid[core, pl.ds(2 * mine, 2)].reshape(64, 1024), hid[1 - core, pl.ds(2 * others, 2)].reshape(64, 1024)],
-                axis=0,
-            )
-            part = jnp.dot(lhs, w[:, lanes], preferred_element_type=F32)
-            keep[s, :, lanes] = part[:64]
-            cs[s, :, lanes] = part[64:]
-            return 0
-
-        lax.fori_loop(0, 4, tile, 0)
+        lhs = jnp.concatenate(
+            [hid[core, pl.ds(2 * mine, 2)].reshape(64, 1024), hid[1 - core, pl.ds(2 * others, 2)].reshape(64, 1024)], axis=0
+        )
+        part = jnp.dot(lhs, w[...], preferred_element_type=F32)
+        cs[s] = part[64:]
+        keep[s] = part[:64]
         c = remote(cs.at[s], cr.at[s], c_ss.at[s], c_rs.at[s], sibling)
         c.start()
         sends.append(c)
@@ -212,36 +220,49 @@
         value = jnp.exp(logits - peak)
         rest = jnp.where(hit, 0.0, value)
         e_all[gz, pair] = rest.astype(BF16)
-        for i, (dx, flip) in enumerate(GROUP):
-            slot = e_all.at[gz, pair]
-            remote(slot, slot, e_ss.at[i], e_rs.at[gz], (z, y, member(dx, flip))).start()
         total = jnp.sum(rest, axis=1, keepdims=True)
         chosen = jnp.sum(jnp.where(hit, value, 0.0), axis=1, keepdims=True)
         lane = lax.broadcasted_iota(I32, (16, 128), 1)
         stat_col[rows, :] = jnp.where(lane == 0, peak, jnp.where(lane == 1, total, jnp.where(lane == 2, chosen, 0.0)))
 
-    for s in range(6):
-        if s < 4:
-            multiply(s)
-        if 1 <= s < 5:
-            pass_on(s - 1)
+    for s in range(4):
+        multiply(s)
+        pass_on(s)
         if s >= 2:
             finish(s - 2)
-
-    def exchange(buf, ss, rs, kind):
+    finish(2)
+    finish(3)
+
+    def give(buf, ss, rs, kind):
         for d in FAR_FIRST:
             c = remote(buf.at[0], buf.at[d], ss.at[d], rs.at[d], along(kind, d))
             c.start()
             sends.append(c)
+
+    def take(buf, rs, kind):
         for d in FAR_FIRST:
             arrived(buf.at[d], rs.at[d], along(kind, d))
         return combine(buf[...])
 
+    def share(j, i, to):
+        c = remote(e_all.at[j], e_all.at[j], e_ss.at[i], e_rs.at[j], (z, y, to))
+        c.start()
+        sends.append(c)
+
     mine = stat_col[...].T[0:8, :]
     st_a[0] = mine
-    peak, total, chosen = exchange(st_a, sa_ss, sa_rs, 0)
+    give(st_a, sa_ss, sa_rs, 0)
+    for dx in (2, 1, 3):
+        share(gz, dx, member(dx, 0))
+    share(gz, 0, member(0, 1))
+    peak, total, chosen = take(st_a, sa_rs, 0)
     st_b[0] = rows_of(peak, total, chosen)
-    peak, total, chosen = exchange(st_b, sb_ss, sb_rs, 1)
+    give(st_b, sb_ss, sb_rs, 1)
+    for dx in (1, 3, 2):
+        j = member(dx, 0)
+        arrived(e_all.at[j], e_rs.at[j], sibling)
+        share(j, 3 + dx, member(0, 1))
+    peak, total, chosen = take(st_b, sb_rs, 1)
     used = lax.broadcasted_iota(I32, (1, 128), 1) < 64
     scale = up_row / jnp.where(used, total + chosen, 1.0)
     st_c[gz] = rows_of(scale * jnp.exp(mine[0:1, :] - peak), -scale * total, tgt_row)
@@ -249,8 +270,8 @@
         c = remote(st_c.at[gz], st_c.at[gz], sc_ss.at[i], sc_rs.at[gz], (z, y, member(dx, flip)))
         c.start()
         sends.append(c)
-    for i, (dx, flip) in enumerate(GROUP):
-        j = member(dx, flip)
+    for dx in range(4):
+        j = member(dx, 1)
         arrived(e_all.at[j], e_rs.at[j], sibling)
     for i, (dx, flip) in enumerate(GROUP):
         j = member(dx, flip)
@@ -271,15 +292,10 @@
         for kind in (0, 1):
             logit_grads(kind, pairs[kind])
 
-        def tile(n, _):
-            lanes = pl.ds(pl.multiple_of(n * 256, 256), 256)
-            lhs = jnp.concatenate([g[kind, pl.ds(2 * pairs[kind], 2)].reshape(64, vocab) for kind in (0, 1)], axis=0)
-            part = lax.dot_general(lhs, w[lanes, :], contract, preferred_element_type=F32).astype(BF16)
-            for kind in (0, 1):
-                p[kind, pl.ds(2 * pairs[kind], 2), :, lanes] = part[64 * kind : 64 * kind + 64].reshape(2, 32, 256)
-            return 0
-
-        lax.fori_loop(0, 4, tile, 0)
+        lhs = jnp.concatenate([g[kind, pl.ds(2 * pairs[kind], 2)].reshape(64, vocab) for kind in (0, 1)], axis=0)
+        part = jnp.dot(lhs, wt[...], preferred_element_type=F32).astype(BF16)
+        for kind in (0, 1):
+            p[kind, pl.ds(2 * pairs[kind], 2)] = part[64 * kind : 64 * kind + 64].reshape(2, 32, 1024)
         for kind in (0, 1):
             if change == 0:
                 chunks = [4 * pairs[kind] + 1 - me[kind]]
@@ -298,12 +314,10 @@
             hid[:, :, :, lanes].reshape(512, 256), g[...].reshape(512, vocab), (((0,), (0,)), ((), ())),
             preferred_element_type=F32,
         )
-        gwv[lanes, :] = part.astype(BF16)
+        gw_ref[lanes, :] = part.astype(BF16)
         return 0
 
     lax.fori_loop(0, 4, weight_tile, 0)
-    store_gw = pltpu.make_async_copy(gwv, gw_hbm, gw_sem)
-    store_gw.start()
 
     for kind in (0, 1):
         for d in range(1, 8):
@@ -329,17 +343,18 @@
 
     for c in sends:
         c.wait_send()
-    for i, (dx, flip) in enumerate(GROUP):
-        remote(e_all.at[gz], e_all.at[gz], e_ss.at[i], e_rs.at[gz], sibling).wait_send()
-    store_gw.wait()
 
 
 def body(hidden_states, weight, targets, upstream):
     vmem = pl.BlockSpec(memory_space=pltpu.VMEM)
-    hbm = pl.BlockSpec(memory_space=pl.ANY)
+    hbm = pl.BlockSpec(memory_space=pltpu.HBM)
     dma = pltpu.SemaphoreType.DMA
     scratch = [
         pltpu.VMEM((1024, 1024), BF16),
+        pltpu.VMEM((1024, 1024), BF16),
+        pltpu.VMEM((8, 1024), BF16),
+        pltpu.VMEM((1, 512), I32),
+        pltpu.VMEM((512,), BF16),
         pltpu.VMEM((2, 8, 32, 1024), BF16),
         pltpu.VMEM((2, 16, 256), BF16),
         pltpu.VMEM((2, 8, 16, 256), BF16),
@@ -354,19 +369,22 @@
         pltpu.VMEM((2, 8, 32, 1024), BF16),
         pltpu.VMEM((2, 8, 16, 256), BF16),
         pltpu.VMEM((2, 8, 16, 256), BF16),
-        pltpu.VMEM((1024, 1024), BF16),
         pltpu.VMEM((128, 128), F32),
         pltpu.VMEM((128, 128), F32),
         pltpu.VMEM((8, 8, 128), F32),
         pltpu.VMEM((8, 8, 128), F32),
         pltpu.VMEM((8, 8, 128), F32),
         pltpu.VMEM((128, 128), F32),
-        dma, dma,
+        dma, dma((3,)),
         dma((2, 8)), dma((2, 8)), dma((2, 8)), dma((2, 8)),
         dma((4,)), dma((4,)), dma((4, 3)), dma((4, 3)),
         dma((7,)), dma((8,)),
         dma((8,)), dma((8,)), dma((8,)), dma((8,)), dma((7,)), dma((8,)),
         dma((2, 8)), dma((2, 8)), dma((2, 8)), dma((2, 8)),
+    ]
+    operands = [
+        pltpu.with_memory_space_constraint(a, pltpu.HBM)
+        for a in (hidden_states, weight, targets.reshape(1, 512), upstream)
     ]
     return pl.pallas_call(
         kernel,
@@ -374,13 +392,13 @@
             jax.ShapeDtypeStruct(hidden_states.shape, BF16),
             jax.ShapeDtypeStruct(weight.shape, BF16),
         ),
-        in_specs=[vmem, hbm, vmem, vmem],
-        out_specs=(vmem, hbm),
+        in_specs=[hbm, hbm, hbm, hbm],
+        out_specs=(vmem, vmem),
         scratch_shapes=scratch,
         name="projection_backward",
         cost_estimate=pl.CostEstimate(flops=3 * 2 * 512 * 1024 * 1024, bytes_accessed=5 << 20, transcendentals=1 << 16),
         compiler_params=pltpu.CompilerParams(collective_id=0, has_side_effects=True, vmem_limit_bytes=48 << 20),
-    )(hidden_states, weight, targets.reshape(1, 512), upstream.reshape(1, 512))
+    )(*operands)
 
 
 def solution(mesh):

time: 92 us -> 78.6 us (0.85)
  Pallas kernels: 85 us -> 75.5 us
  local copies, waits for them, and re-layouts: 5.6 us -> 1.93 us
    pallas_call x1, Pallas kernels: 85 us -> 75.5 us  [body(): pl.pallas_call(kernel, out_shape=(jax.ShapeDtypeStruct(hidden_states.shap...]
    unnamed x8 -> x2, local copies, waits for them, and re-layouts: 4.91 us -> 1.93 us
where the time goes in v2:
time: 78.6 us; the launch traced here: 78.1 us
  Pallas kernels  75.5 us (96%)
  local copies, waits for them, and re-layouts  1.93 us (2%)
    pallas_call x1, Pallas kernels, body(): pl.pallas_call(kernel, out_shape=(jax.ShapeDtypeStruct(hidden_states.shap...  75.5 us
    unnamed x2, local copies, waits for them, and re-layouts  1.93 us

profile of v2, /device:TPU:1, one launch (start us, length us, event | category | flops | bytes accessed | tf_op | source)
XLA Modules:
  0.0 78.1 jit_solution(2612274591405338176)
XLA Ops:
  0.6 75.5 %projection_backward.1 = (bf16[8,1024]{1,0:T(8,128)(2,1)S(1)}, bf16[1024,1024]{1,0:T(8,128)(2,1)S(1)}) custom-call(bf16[8,1024]{1,0:T(8,128)(2,1)} %h_hbm.1, bf16[1024,1024]{1,0:T(8,128)(2,1)} %w_hbm.1, s32[1,512]{1,0:T(1,128)} %bitcast.1, bf16[512]{0:T(512)(128)(2,1)} %up_hbm.1), custom_call_target="tpu_custom_call" | custom-call | flops 3221225472 | bytes 5242880 | tf_op jit(solution)/shard_map/projection_backward/pallas_call | solution.py:389
  76.2 0.6 copy.8
  76.8 1.3 %copy.9 = bf16[1024,1024]{1,0:T(8,128)(2,1)} copy(bf16[1024,1024]{1,0:T(8,128)(2,1)S(1)} %get-tuple-element.5) | data formatting | bytes 4194304

commit v3 on v2

--- a/solution.py
+++ b/solution.py
@@ -62,14 +62,16 @@
 def kernel(
     h_hbm, w_hbm, tgt_hbm, up_hbm, gh_ref, gw_ref,
     w, wt, h_ref, tgt_ref, up_ref, hid, a1s, a1r, keep, cs, cr, xs, xr, e_all, g, p, r1, s2, r2,
-    own_col, stat_col, st_a, st_b, st_c, t_col,
-    w_sem, in_sem, a1_ss, a1_rs, a2_ss, a2_rs, c_ss, c_rs, x_ss, x_rs,
-    e_ss, e_rs, sa_ss, sa_rs, sb_ss, sb_rs, sc_ss, sc_rs, d1_ss, d1_rs, d2_ss, d2_rs,
+    tp, tr, tg, th, own_col, all_col, stat_col, st_a, st_b, st_c, t_col, d_col,
+    w_sem, in_sem, a1_ss, a1_rs, a2_ss, a2_rs, a2_hs, c_ss, c_rs, x_ss, x_rs,
+    e_ss, e_rs, sa_ss, sa_rs, sb_ss, sb_rs, sc_ss, sc_rs, t_ss, t_rs, d1_ss, d1_rs, d2_ss, d2_rs,
 ):
     z, y, gz = lax.axis_index("gx"), lax.axis_index("gy"), lax.axis_index("gz")
     xx, core = gz // 2, gz % 2
     vocab = w.shape[1]
     zp, yp = z // 2, y // 2
+    first_column = (z * 8 + y) * vocab
+    contract = (((1,), (1,)), ((), ()))
     me = (z, y)
 
     def along(kind, d):
@@ -102,6 +104,18 @@
     a1s[1] = high.astype(BF16)
     a1r[0, y] = low.astype(BF16)
     a1r[1, z] = high.astype(BF16)
+
+    pl.semaphore_wait(barrier, 21)
+
+    sends = []
+    for d in FAR_FIRST:
+        for kind in (0, 1):
+            c = remote(a1s.at[kind], a1r.at[kind, me[1 - kind]], a1_ss.at[kind, d], a1_rs.at[kind, me[1 - kind]], along(kind, d))
+            c.start()
+            sends.append(c)
+
+    def arrived(dst, sem, peer):
+        remote(dst, dst, sem, sem, peer).wait_recv()
 
     k = lax.broadcasted_iota(I32, (128, 512), 0)
     t = lax.broadcasted_iota(I32, (128, 512), 1)
@@ -116,12 +130,16 @@
     values = jnp.where(sub == 0, jnp.broadcast_to((tgt >> 8).astype(F32), (128, 512)), 0.0)
     values = jnp.where(sub == 1, jnp.broadcast_to((tgt & 255).astype(F32), (128, 512)), values)
     values = jnp.where(sub == 2, jnp.broadcast_to(up_ref[...].reshape(1, 512).astype(F32), (128, 512)), values).astype(BF16)
-    contract = (((1,), (1,)), ((), ()))
     own_col[...] = lax.dot_general(select, values, contract, preferred_element_type=F32)
     own_row = lax.dot_general(values, select, contract, preferred_element_type=F32)
     tgt_row = own_row[0:1, :] * 256.0 + own_row[1:2, :]
     up_row = own_row[2:3, :]
     stat_col[...] = jnp.zeros((128, 128), F32)
+    row = lax.broadcasted_iota(I32, (512, 128), 0)
+    first, second = (row >> 5) & 7, (row & 31) >> 2
+    token = jnp.where(row < 256, first * 64 + second * 8, second * 64 + first * 8 + 4) + (row & 3)
+    order = (token[:, 0:1] == lax.broadcasted_iota(I32, (512, 512), 1)).astype(F32).astype(BF16)
+    all_col[...] = lax.dot_general(order, values, contract, preferred_element_type=F32)
     load_w.wait()
 
     def turn(n, _):
@@ -131,17 +149,41 @@
 
     lax.fori_loop(0, 4, turn, 0)
 
-    pl.semaphore_wait(barrier, 21)
-
-    sends = []
-    for d in FAR_FIRST:
+    def chosen_rows(b, _):
+        info = all_col[pl.ds(pl.multiple_of(b * 128, 128), 128), :]
+        target = info[:, 0:1] * 256.0 + info[:, 1:2]
+        hit = ((lax.broadcasted_iota(I32, (128, vocab), 1) + first_column).astype(F32) == target).astype(F32)
+        part = jnp.dot(hit.astype(BF16), wt[...], preferred_element_type=F32).astype(BF16)
+        tp[b // 2, pl.ds((b % 2) * 4, 4)] = part.reshape(4, 32, 1024)
+        return 0
+
+    lax.fori_loop(0, 4, chosen_rows, 0)
+
+    def send_chosen(kind, src, dst, i, d):
+        c = remote(src, dst, t_ss.at[kind, i], t_rs.at[kind, i], along(1 - kind, d))
+        c.start()
+        sends.append(c)
+
+    for kind in (0, 1):
+        for h, d in enumerate((1, 7)):
+            half = pl.ds(16 * h, 16)
+            send_chosen(kind, tp.at[kind, (me[kind] + 4) % 8, half], th.at[kind, h], 4 + h, 2 * d)
+            send_chosen(kind, tp.at[kind, (me[kind] + 3 * d) % 8], tg.at[kind, h], 2 + h, d)
+            send_chosen(kind, tp.at[kind, (me[kind] + d) % 8], tr.at[kind, h], h, d)
+
+    def join_chosen():
         for kind in (0, 1):
-            c = remote(a1s.at[kind], a1r.at[kind, me[1 - kind]], a1_ss.at[kind, d], a1_rs.at[kind, me[1 - kind]], along(kind, d))
-            c.start()
-            sends.append(c)
-
-    def arrived(dst, sem, peer):
-        remote(dst, dst, sem, sem, peer).wait_recv()
+            for h, d in enumerate((1, 7)):
+                arrived(tg.at[kind, h], t_rs.at[kind, 2 + h], along(1 - kind, 1))
+                arrived(th.at[kind, h], t_rs.at[kind, 4 + h], along(1 - kind, 1))
+                q = (me[kind] + 2 * d) % 8
+                for b in (0, 1):
+                    rows = pl.ds(16 * b, 16)
+                    total = tp[kind, q, rows, :].astype(F32) + tg[kind, h, rows, :].astype(F32)
+                    if b == h:
+                        total = total + th[kind, h].astype(F32)
+                    tp[kind, q, rows, :] = total.astype(BF16)
+                send_chosen(kind, tp.at[kind, q], tr.at[kind, 2 + h], 6 + h, 2 * d)
 
     for kind in (0, 1):
         mine = me[1 - kind]
@@ -153,7 +195,7 @@
                 unpack(a1r[kind, 4 * b + 2 * q].astype(F32), a1r[kind, 4 * b + 2 * q + 1].astype(F32)) for q in range(2)
             ]
             hid[kind, me[kind], 16 * b : 16 * b + 16, :] = jnp.concatenate(rows, axis=0).astype(BF16)
-        for d in (1, 7, 2, 6, 3, 5, 4):
+        for d in (2, 6, 1, 7):
             slot = hid.at[kind, me[kind]]
             c = remote(slot, slot, a2_ss.at[kind, d], a2_rs.at[kind, me[kind]], along(1 - kind, d))
             c.start()
@@ -173,15 +215,28 @@
 
     sibling = (z, y, member(0, 1))
 
+    def relay():
+        for kind in (0, 1):
+            for h, d in enumerate((1, 7)):
+                q = (me[kind] - 2 * d) % 8
+                slot = hid.at[kind, q]
+                arrived(slot, a2_rs.at[kind, q], along(1 - kind, 1))
+                c = remote(slot, slot, a2_ss.at[kind, 3 + 2 * h], a2_rs.at[kind, q], along(1 - kind, d))
+                c.start()
+                sends.append(c)
+                half = hid.at[kind, q, 16 * h : 16 * h + 16]
+                c = remote(half, half, a2_ss.at[kind, 4 * h], a2_hs.at[kind, h], along(1 - kind, 2 * d))
+                c.start()
+                sends.append(c)
+
     def multiply(s):
         for kind in (0, 1):
-            pair = pair_of(kind, s)
-            if s == 0:
-                chunks = [4 * pair + 1 - me[kind]]
-            else:
-                chunks = [2 * pair, 2 * pair + 1]
-            for q in chunks:
-                arrived(hid.at[kind, q], a2_rs.at[kind, q], along(1 - kind, 1))
+            q = 2 * pair_of(kind, s) + 1 - me[kind] % 2
+            arrived(hid.at[kind, q], a2_rs.at[kind, q], along(1 - kind, 1))
+            if s == 3:
+                q = (me[kind] + 4) % 8
+                for h in (0, 1):
+                    arrived(hid.at[kind, q, 16 * h : 16 * h + 16], a2_hs.at[kind, h], along(1 - kind, 1))
         mine, others = own_pair(s), other_pair(s)
 
         lhs = jnp.concatenate(
@@ -214,99 +269,167 @@
         rows = pl.ds(pl.multiple_of(pair * 16, 16), 16)
         info = own_col[rows, :]
         target = info[:, 0:1] * 256.0 + info[:, 1:2]
-        column = lax.broadcasted_iota(I32, (16, vocab), 1) + (z * 8 + y) * vocab
+        column = lax.broadcasted_iota(I32, (16, vocab), 1) + first_column
         hit = column.astype(F32) == target
         peak = jnp.max(logits, axis=1, keepdims=True)
         value = jnp.exp(logits - peak)
         rest = jnp.where(hit, 0.0, value)
         e_all[gz, pair] = rest.astype(BF16)
+        for dx in (2, 1, 3):
+            share(gz, pair, s, dx, member(dx, 0))
+        share(gz, pair, s, 0, member(0, 1))
         total = jnp.sum(rest, axis=1, keepdims=True)
         chosen = jnp.sum(jnp.where(hit, value, 0.0), axis=1, keepdims=True)
         lane = lax.broadcasted_iota(I32, (16, 128), 1)
         stat_col[rows, :] = jnp.where(lane == 0, peak, jnp.where(lane == 1, total, jnp.where(lane == 2, chosen, 0.0)))
 
-    for s in range(4):
-        multiply(s)
-        pass_on(s)
-        if s >= 2:
-            finish(s - 2)
-    finish(2)
-    finish(3)
-
-    def give(buf, ss, rs, kind):
-        for d in FAR_FIRST:
-            c = remote(buf.at[0], buf.at[d], ss.at[d], rs.at[d], along(kind, d))
-            c.start()
-            sends.append(c)
-
-    def take(buf, rs, kind):
-        for d in FAR_FIRST:
-            arrived(buf.at[d], rs.at[d], along(kind, d))
-        return combine(buf[...])
-
-    def share(j, i, to):
-        c = remote(e_all.at[j], e_all.at[j], e_ss.at[i], e_rs.at[j], (z, y, to))
+    def share(j, pair, s, i, to):
+        slot = e_all.at[j, pair]
+        c = remote(slot, slot, e_ss.at[i, s], e_rs.at[j, pair], (z, y, to))
         c.start()
         sends.append(c)
 
-    mine = stat_col[...].T[0:8, :]
-    st_a[0] = mine
-    give(st_a, sa_ss, sa_rs, 0)
-    for dx in (2, 1, 3):
-        share(gz, dx, member(dx, 0))
-    share(gz, 0, member(0, 1))
-    peak, total, chosen = take(st_a, sa_rs, 0)
-    st_b[0] = rows_of(peak, total, chosen)
-    give(st_b, sb_ss, sb_rs, 1)
-    for dx in (1, 3, 2):
-        j = member(dx, 0)
-        arrived(e_all.at[j], e_rs.at[j], sibling)
-        share(j, 3 + dx, member(0, 1))
-    peak, total, chosen = take(st_b, sb_rs, 1)
-    used = lax.broadcasted_iota(I32, (1, 128), 1) < 64
-    scale = up_row / jnp.where(used, total + chosen, 1.0)
-    st_c[gz] = rows_of(scale * jnp.exp(mine[0:1, :] - peak), -scale * total, tgt_row)
-    for i, (dx, flip) in enumerate(GROUP):
-        c = remote(st_c.at[gz], st_c.at[gz], sc_ss.at[i], sc_rs.at[gz], (z, y, member(dx, flip)))
-        c.start()
-        sends.append(c)
-    for dx in range(4):
-        j = member(dx, 1)
-        arrived(e_all.at[j], e_rs.at[j], sibling)
-    for i, (dx, flip) in enumerate(GROUP):
-        j = member(dx, flip)
-        arrived(st_c.at[j], sc_rs.at[j], sibling)
-    t_col[...] = jnp.concatenate([st_c[...].reshape(64, 128), jnp.zeros((64, 128), F32)], axis=0).T
-
-    def logit_grads(kind, pair):
-        column = (lax.broadcasted_iota(I32, (16, vocab), 1) + (z * 8 + y) * vocab).astype(F32)
-        info = t_col[pl.ds(pl.multiple_of(pair * 16, 16), 16), :]
-        for x in range(4):
-            j = 2 * x + kind
-            value = info[:, 8 * j : 8 * j + 1] * e_all[j, pair].astype(F32)
-            value = jnp.where(column == info[:, 8 * j + 2 : 8 * j + 3], info[:, 8 * j + 1 : 8 * j + 2], value)
-            g[kind, 2 * pair + x // 2, 16 * (x % 2) : 16 * (x % 2) + 16, :] = value.astype(BF16)
-
-    for step, change in enumerate((2, 1, 3, 0)):
-        pairs = ((zp + change) % 4, (yp + change) % 4)
-        for kind in (0, 1):
-            logit_grads(kind, pairs[kind])
-
-        lhs = jnp.concatenate([g[kind, pl.ds(2 * pairs[kind], 2)].reshape(64, vocab) for kind in (0, 1)], axis=0)
+    def forward(s):
+        for dx in (1, 3, 2):
+            j, pair = member(dx, 0), own_pair(s)
+            arrived(e_all.at[j, pair], e_rs.at[j, pair], sibling)
+            share(j, pair, s, 3 + dx, member(0, 1))
+
+    def scatter(kind, s):
+        pair = pair_of(kind, s)
+        if s == 0:
+            chunks = [4 * pair + 1 - me[kind]]
+            r1[kind, me[kind]] = p[kind, me[kind]]
+        else:
+            chunks = [2 * pair, 2 * pair + 1]
+        for i, q in enumerate(chunks):
+            to = (q, y, gz) if kind == 0 else (z, q, gz)
+            c = remote(
+                p.at[kind, q], r1.at[kind, me[kind]], d1_ss.at[kind, 2 * s + i], d1_rs.at[kind, me[kind]], to
+            )
+            c.start()
+            sends.append(c)
+
+    def terms(s):
+        pairs = (pair_of(0, s), pair_of(1, s))
+        for dx in range(4):
+            j, pair = member(dx, 1), other_pair(s)
+            arrived(e_all.at[j, pair], e_rs.at[j, pair], sibling)
+        lhs = jnp.concatenate([e_all[2 * x + kind, pairs[kind]] for kind in (0, 1) for x in range(4)], axis=0)
         part = jnp.dot(lhs, wt[...], preferred_element_type=F32).astype(BF16)
         for kind in (0, 1):
             p[kind, pl.ds(2 * pairs[kind], 2)] = part[64 * kind : 64 * kind + 64].reshape(2, 32, 1024)
-        for kind in (0, 1):
-            if change == 0:
-                chunks = [4 * pairs[kind] + 1 - me[kind]]
-                r1[kind, me[kind]] = p[kind, me[kind]]
-            else:
-                chunks = [2 * pairs[kind], 2 * pairs[kind] + 1]
-            for i, q in enumerate(chunks):
-                to = (q, y, gz) if kind == 0 else (z, q, gz)
-                c = remote(p.at[kind, q], r1.at[kind, me[kind]], d1_ss.at[kind, 2 * step + i], d1_rs.at[kind, me[kind]], to)
-                c.start()
-                sends.append(c)
+            scatter(kind, s)
+
+    def stat_peer(phase, d):
+        over_z = core == phase
+        return (jnp.where(over_z, (z + d) % 8, z), jnp.where(over_z, y, (y + d) % 8), gz)
+
+    def give(buf, ss, rs, phase):
+        for d in FAR_FIRST:
+            c = remote(buf.at[0], buf.at[d], ss.at[d], rs.at[d], stat_peer(phase, d))
+            c.start()
+            sends.append(c)
+
+    def take(buf, rs, phase):
+        for d in FAR_FIRST:
+            arrived(buf.at[d], rs.at[d], stat_peer(phase, d))
+        return combine(buf[...])
+
+    def stats_first():
+        st_a[0] = stat_col[...].T[0:8, :]
+        give(st_a, sa_ss, sa_rs, 0)
+
+    def stats_second():
+        st_b[0] = rows_of(*take(st_a, sa_rs, 0))
+        give(st_b, sb_ss, sb_rs, 1)
+
+    def stats_third():
+        peak, total, chosen = take(st_b, sb_rs, 1)
+        used = lax.broadcasted_iota(I32, (1, 128), 1) < 64
+        scale = up_row / jnp.where(used, total + chosen, 1.0)
+        factors = [scale * jnp.exp(st_a[d, 0:1, :] - peak) for d in range(8)]
+        st_c[gz, 0:8] = rows_of(factors[0], -scale * total, tgt_row)
+        st_c[gz, 8:16] = rows_of(*factors)
+        for i, (dx, flip) in enumerate(GROUP):
+            c = remote(st_c.at[gz], st_c.at[gz], sc_ss.at[i], sc_rs.at[gz], (z, y, member(dx, flip)))
+            c.start()
+            sends.append(c)
+
+    multiply(0)
+    relay()
+    pass_on(0)
+    multiply(1)
+    pass_on(1)
+    multiply(2)
+    finish(0)
+    pass_on(2)
+    finish(1)
+    multiply(3)
+    join_chosen()
+    forward(0)
+    pass_on(3)
+    finish(2)
+    terms(0)
+    forward(1)
+    terms(1)
+    finish(3)
+    stats_first()
+    forward(2)
+    terms(2)
+    forward(3)
+    stats_second()
+    terms(3)
+
+    for kind in (0, 1):
+        for i in (0, 1, 2, 3):
+            arrived(tr.at[kind, i], t_rs.at[kind, (0, 1, 6, 7)[i]], along(1 - kind, 1))
+        total = tp[kind, me[kind]].astype(F32)
+        for i in range(4):
+            total = total + tr[kind, i].astype(F32)
+        tp[kind, me[kind]] = total.astype(BF16)
+
+    stats_third()
+    for dx, flip in GROUP:
+        j = member(dx, flip)
+        arrived(st_c.at[j], sc_rs.at[j], sibling)
+
+    owners = [4 * (me[kind] % 2) + 2 * h + kind for kind in (0, 1) for h in (0, 1)]
+    d_col[...] = jnp.concatenate([st_c[j] for j in owners] + [jnp.zeros((64, 128), F32)], axis=0).T
+    for kind in (0, 1):
+        for d in range(1, 8):
+            src = (me[kind] + d) % 8
+            arrived(r1.at[kind, src], d1_rs.at[kind, src], along(1 - kind, 1))
+        info = d_col[pl.ds(pl.multiple_of(me[kind] // 2 * 16, 16), 16), :]
+        for b in range(2):
+            first = 32 * kind + 16 * b
+            rows = info[:, first + 1 : first + 2] * tp[kind, me[kind], 16 * b : 16 * b + 16, :].astype(F32)
+            for d in range(8):
+                part = r1[kind, (me[kind] + 8 - d) % 8, 16 * b : 16 * b + 16, :].astype(F32)
+                rows = rows + info[:, first + 8 + d : first + 9 + d] * part
+            for q in range(2):
+                low, high = pack(rows[8 * q : 8 * q + 8])
+                s2[kind, 4 * b + 2 * q] = low.astype(BF16)
+                s2[kind, 4 * b + 2 * q + 1] = high.astype(BF16)
+        for d in FAR_FIRST:
+            to = (me[1 - kind] + d) % 8
+            c = remote(s2.at[kind, to], r2.at[kind, d], d2_ss.at[kind, d], d2_rs.at[kind, d], along(kind, d))
+            c.start()
+            sends.append(c)
+
+    t_col[...] = st_c[...].reshape(128, 128).T
+
+    def logit_grads(pair, _):
+        column = (lax.broadcasted_iota(I32, (16, vocab), 1) + first_column).astype(F32)
+        info = t_col[pl.ds(pl.multiple_of(pair * 16, 16), 16), :]
+        for j in range(8):
+            kind, x = j % 2, j // 2
+            value = info[:, 16 * j : 16 * j + 1] * e_all[j, pair].astype(F32)
+            value = jnp.where(column == info[:, 16 * j + 2 : 16 * j + 3], info[:, 16 * j + 1 : 16 * j + 2], value)
+            g[kind, 2 * pair + x // 2, 16 * (x % 2) : 16 * (x % 2) + 16, :] = value.astype(BF16)
+        return 0
+
+    lax.fori_loop(0, 4, logit_grads, 0)
 
     def weight_tile(n, _):
         lanes = pl.ds(pl.multiple_of(n * 256, 256), 256)
@@ -319,21 +442,6 @@
 
     lax.fori_loop(0, 4, weight_tile, 0)
 
-    for kind in (0, 1):
-        for d in range(1, 8):
-            src = (me[kind] + d) % 8
-            arrived(r1.at[kind, src], d1_rs.at[kind, src], along(1 - kind, 1))
-        for b in range(2):
-            rows = sum(r1[kind, src, 16 * b : 16 * b + 16, :].astype(F32) for src in range(8))
-            for q in range(2):
-                low, high = pack(rows[8 * q : 8 * q + 8])
-                s2[kind, 4 * b + 2 * q] = low.astype(BF16)
-                s2[kind, 4 * b + 2 * q + 1] = high.astype(BF16)
-        for d in FAR_FIRST:
-            to = (me[1 - kind] + d) % 8
-            c = remote(s2.at[kind, to], r2.at[kind, d], d2_ss.at[kind, d], d2_rs.at[kind, d], along(kind, d))
-            c.start()
-            sends.append(c)
     halves = []
     for kind in (0, 1):
         for d in FAR_FIRST:
@@ -369,18 +477,24 @@
         pltpu.VMEM((2, 8, 32, 1024), BF16),
         pltpu.VMEM((2, 8, 16, 256), BF16),
         pltpu.VMEM((2, 8, 16, 256), BF16),
+        pltpu.VMEM((2, 8, 32, 1024), BF16),
+        pltpu.VMEM((2, 4, 32, 1024), BF16),
+        pltpu.VMEM((2, 2, 32, 1024), BF16),
+        pltpu.VMEM((2, 2, 16, 1024), BF16),
         pltpu.VMEM((128, 128), F32),
+        pltpu.VMEM((512, 128), F32),
         pltpu.VMEM((128, 128), F32),
         pltpu.VMEM((8, 8, 128), F32),
         pltpu.VMEM((8, 8, 128), F32),
-        pltpu.VMEM((8, 8, 128), F32),
+        pltpu.VMEM((8, 16, 128), F32),
+        pltpu.VMEM((128, 128), F32),
         pltpu.VMEM((128, 128), F32),
         dma, dma((3,)),
-        dma((2, 8)), dma((2, 8)), dma((2, 8)), dma((2, 8)),
+        dma((2, 8)), dma((2, 8)), dma((2, 8)), dma((2, 8)), dma((2, 2)),
         dma((4,)), dma((4,)), dma((4, 3)), dma((4, 3)),
-        dma((7,)), dma((8,)),
+        dma((7, 4)), dma((8, 4)),
         dma((8,)), dma((8,)), dma((8,)), dma((8,)), dma((7,)), dma((8,)),
-        dma((2, 8)), dma((2, 8)), dma((2, 8)), dma((2, 8)),
+        dma((2, 8)), dma((2, 8)), dma((2, 8)), dma((2, 8)), dma((2, 8)), dma((2, 8)),
     ]
     operands = [
         pltpu.with_memory_space_constraint(a, pltpu.HBM)

time: 78.6 us -> 75.1 us (0.955)
  Pallas kernels: 75.5 us -> 72.3 us
    pallas_call x1, Pallas kernels: 75.5 us -> 72.3 us  [body(): pl.pallas_call(kernel, out_shape=(jax.ShapeDtypeStruct(hidden_states.shap...]
where the time goes in v3:
time: 75.1 us; the launch traced here: 74.9 us
  Pallas kernels  72.3 us (96%)
  local copies, waits for them, and re-layouts  1.93 us (3%)
    pallas_call x1, Pallas kernels, body(): pl.pallas_call(kernel, out_shape=(jax.ShapeDtypeStruct(hidden_states.shap...  72.3 us
    unnamed x2, local copies, waits for them, and re-layouts  1.93 us

profile of v3, /device:TPU:1, one launch (start us, length us, event | category | flops | bytes accessed | tf_op | source)
XLA Modules:
  0.0 74.9 jit_solution(8208954854285590781)
XLA Ops:
  0.6 72.3 %projection_backward.1 = (bf16[8,1024]{1,0:T(8,128)(2,1)S(1)}, bf16[1024,1024]{1,0:T(8,128)(2,1)S(1)}) custom-call(bf16[8,1024]{1,0:T(8,128)(2,1)} %h_hbm.1, bf16[1024,1024]{1,0:T(8,128)(2,1)} %w_hbm.1, s32[1,512]{1,0:T(1,128)} %bitcast.1, bf16[512]{0:T(512)(128)(2,1)} %up_hbm.1), custom_call_target="tpu_custom_call" | custom-call | flops 3221225472 | bytes 5242880 | tf_op jit(solution)/shard_map/projection_backward/pallas_call | solution.py:503
  73.0 0.6 copy.8
  73.6 1.3 %copy.9 = bf16[1024,1024]{1,0:T(8,128)(2,1)} copy(bf16[1024,1024]{1,0:T(8,128)(2,1)S(1)} %get-tuple-element.5) | data formatting | bytes 4194304

commit v4 on v3

--- a/solution.py
+++ b/solution.py
@@ -164,12 +164,13 @@
         c.start()
         sends.append(c)
 
-    for kind in (0, 1):
-        for h, d in enumerate((1, 7)):
-            half = pl.ds(16 * h, 16)
-            send_chosen(kind, tp.at[kind, (me[kind] + 4) % 8, half], th.at[kind, h], 4 + h, 2 * d)
-            send_chosen(kind, tp.at[kind, (me[kind] + 3 * d) % 8], tg.at[kind, h], 2 + h, d)
-            send_chosen(kind, tp.at[kind, (me[kind] + d) % 8], tr.at[kind, h], h, d)
+    def spread_chosen():
+        for kind in (0, 1):
+            for h, d in enumerate((1, 7)):
+                half = pl.ds(16 * h, 16)
+                send_chosen(kind, tp.at[kind, (me[kind] + 4) % 8, half], th.at[kind, h], 4 + h, 2 * d)
+                send_chosen(kind, tp.at[kind, (me[kind] + 3 * d) % 8], tg.at[kind, h], 2 + h, d)
+                send_chosen(kind, tp.at[kind, (me[kind] + d) % 8], tr.at[kind, h], h, d)
 
     def join_chosen():
         for kind in (0, 1):
@@ -361,13 +362,13 @@
     pass_on(0)
     multiply(1)
     pass_on(1)
+    finish(0)
     multiply(2)
-    finish(0)
     pass_on(2)
     finish(1)
+    forward(0)
     multiply(3)
-    join_chosen()
-    forward(0)
+    spread_chosen()
     pass_on(3)
     finish(2)
     terms(0)
@@ -375,10 +376,11 @@
     terms(1)
     finish(3)
     stats_first()
+    join_chosen()
     forward(2)
     terms(2)
+    stats_second()
     forward(3)
-    stats_second()
     terms(3)
 
     for kind in (0, 1):

time: 75.1 us -> 71.7 us (0.955)
  Pallas kernels: 72.3 us -> 69 us
    pallas_call x1, Pallas kernels: 72.3 us -> 69 us  [body(): pl.pallas_call(kernel, out_shape=(jax.ShapeDtypeStruct(hidden_states.shap...]
where the time goes in v4:
time: 71.7 us; the launch traced here: 71.5 us
  Pallas kernels  69 us (96%)
  local copies, waits for them, and re-layouts  1.93 us (3%)
    pallas_call x1, Pallas kernels, body(): pl.pallas_call(kernel, out_shape=(jax.ShapeDtypeStruct(hidden_states.shap...  69 us
    unnamed x2, local copies, waits for them, and re-layouts  1.93 us

profile of v4, /device:TPU:1, one launch (start us, length us, event | category | flops | bytes accessed | tf_op | source)
XLA Modules:
  0.0 71.5 jit_solution(995025097745002881)
XLA Ops:
  0.6 69.0 %projection_backward.1 = (bf16[8,1024]{1,0:T(8,128)(2,1)S(1)}, bf16[1024,1024]{1,0:T(8,128)(2,1)S(1)}) custom-call(bf16[8,1024]{1,0:T(8,128)(2,1)} %h_hbm.1, bf16[1024,1024]{1,0:T(8,128)(2,1)} %w_hbm.1, s32[1,512]{1,0:T(1,128)} %bitcast.1, bf16[512]{0:T(512)(128)(2,1)} %up_hbm.1), custom_call_target="tpu_custom_call" | custom-call | flops 3221225472 | bytes 5242880 | tf_op jit(solution)/shard_map/projection_backward/pallas_call | solution.py:505
  69.6 0.6 copy.8
  70.2 1.3 %copy.9 = bf16[1024,1024]{1,0:T(8,128)(2,1)} copy(bf16[1024,1024]{1,0:T(8,128)(2,1)S(1)} %get-tuple-element.5) | data formatting | bytes 4194304

commit v5 on v4

--- a/solution.py
+++ b/solution.py
@@ -245,22 +245,22 @@
         )
         part = jnp.dot(lhs, w[...], preferred_element_type=F32)
         cs[s] = part[64:]
-        keep[s] = part[:64]
         c = remote(cs.at[s], cr.at[s], c_ss.at[s], c_rs.at[s], sibling)
         c.start()
         sends.append(c)
+        keep[s] = part[:64]
 
     def pass_on(s):
         arrived(cr.at[s], c_rs.at[s], sibling)
-        xs[s] = keep[s] + cr[s]
-        for dx in (2, 1, 3):
-            to = (xx + dx) % 4
-            c = remote(
-                xs.at[s, pl.ds(pl.multiple_of(to * 16, 16), 16)], xr.at[s, dx - 1], x_ss.at[s, dx - 1], x_rs.at[s, dx - 1],
-                (z, y, member(dx, 0)),
-            )
-            c.start()
-            sends.append(c)
+        for dx in (2, 1, 3, 0):
+            rows = pl.ds(pl.multiple_of((xx + dx) % 4 * 16, 16), 16)
+            xs[s, rows, :] = keep[s, rows, :] + cr[s, rows, :]
+            if dx:
+                c = remote(
+                    xs.at[s, rows], xr.at[s, dx - 1], x_ss.at[s, dx - 1], x_rs.at[s, dx - 1], (z, y, member(dx, 0))
+                )
+                c.start()
+                sends.append(c)
 
     def finish(s):
         for dx in (2, 1, 3):
@@ -376,12 +376,14 @@
     terms(1)
     finish(3)
     stats_first()
+    forward(2)
     join_chosen()
-    forward(2)
     terms(2)
     stats_second()
     forward(3)
     terms(3)
+
+    stats_third()
 
     for kind in (0, 1):
         for i in (0, 1, 2, 3):
@@ -391,7 +393,6 @@
             total = total + tr[kind, i].astype(F32)
         tp[kind, me[kind]] = total.astype(BF16)
 
-    stats_third()
     for dx, flip in GROUP:
         j = member(dx, flip)
         arrived(st_c.at[j], sc_rs.at[j], sibling)
@@ -444,6 +445,9 @@
 
     lax.fori_loop(0, 4, weight_tile, 0)
 
+    finished = sends[:-14]
+    for c in finished:
+        c.wait_send()
     halves = []
     for kind in (0, 1):
         for d in FAR_FIRST:
@@ -451,7 +455,7 @@
         halves.append(s2[kind, me[1 - kind]].astype(F32) + sum(r2[kind, d].astype(F32) for d in range(1, 8)))
     gh_ref[...] = unpack(*halves).astype(BF16)
 
-    for c in sends:
+    for c in sends[-14:]:
         c.wait_send()
 
 

time: 71.7 us -> 71.4 us (level)
  no operation moved by 1% of the time
where the time goes in v5:
time: 71.4 us; the launch traced here: 71.2 us
  Pallas kernels  68.6 us (96%)
  local copies, waits for them, and re-layouts  1.93 us (3%)
    pallas_call x1, Pallas kernels, body(): pl.pallas_call(kernel, out_shape=(jax.ShapeDtypeStruct(hidden_states.shap...  68.6 us
    unnamed x2, local copies, waits for them, and re-layouts  1.93 us

profile of v5, /device:TPU:1, one launch (start us, length us, event | category | flops | bytes accessed | tf_op | source)
XLA Modules:
  0.0 71.2 jit_solution(3665150593880342842)
XLA Ops:
  0.6 68.6 %projection_backward.1 = (bf16[8,1024]{1,0:T(8,128)(2,1)S(1)}, bf16[1024,1024]{1,0:T(8,128)(2,1)S(1)}) custom-call(bf16[8,1024]{1,0:T(8,128)(2,1)} %h_hbm.1, bf16[1024,1024]{1,0:T(8,128)(2,1)} %w_hbm.1, s32[1,512]{1,0:T(1,128)} %bitcast.1, bf16[512]{0:T(512)(128)(2,1)} %up_hbm.1), custom_call_target="tpu_custom_call" | custom-call | flops 3221225472 | bytes 5242880 | tf_op jit(solution)/shard_map/projection_backward/pallas_call | solution.py:509
  69.3 0.6 copy.8
  69.9 1.3 %copy.9 = bf16[1024,1024]{1,0:T(8,128)(2,1)} copy(bf16[1024,1024]{1,0:T(8,128)(2,1)S(1)} %get-tuple-element.5) | data formatting | bytes 4194304

commit v6 on v5

--- a/solution.py
+++ b/solution.py
@@ -157,8 +157,6 @@
         tp[b // 2, pl.ds((b % 2) * 4, 4)] = part.reshape(4, 32, 1024)
         return 0
 
-    lax.fori_loop(0, 4, chosen_rows, 0)
-
     def send_chosen(kind, src, dst, i, d):
         c = remote(src, dst, t_ss.at[kind, i], t_rs.at[kind, i], along(1 - kind, d))
         c.start()
@@ -201,6 +199,8 @@
             c = remote(slot, slot, a2_ss.at[kind, d], a2_rs.at[kind, me[kind]], along(1 - kind, d))
             c.start()
             sends.append(c)
+
+    lax.fori_loop(0, 4, chosen_rows, 0)
 
     def shift(s, parity):
         return (0, 2 * parity + 3, 5 - 2 * parity, 2)[s]
@@ -357,8 +357,8 @@
             c.start()
             sends.append(c)
 
+    relay()
     multiply(0)
-    relay()
     pass_on(0)
     multiply(1)
     pass_on(1)

time: 71.4 us -> 72.4 us (1.014)
  Pallas kernels: 68.6 us -> 69.6 us
    pallas_call x1, Pallas kernels: 68.6 us -> 69.6 us  [body(): pl.pallas_call(kernel, out_shape=(jax.ShapeDtypeStruct(hidden_states.shap...]
where the time goes in v6:
time: 72.4 us; the launch traced here: 72.1 us
  Pallas kernels  69.6 us (96%)
  local copies, waits for them, and re-layouts  1.93 us (3%)
    pallas_call x1, Pallas kernels, body(): pl.pallas_call(kernel, out_shape=(jax.ShapeDtypeStruct(hidden_states.shap...  69.6 us
    unnamed x2, local copies, waits for them, and re-layouts  1.93 us

profile of v6, /device:TPU:1, one launch (start us, length us, event | category | flops | bytes accessed | tf_op | source)
XLA Modules:
  0.0 72.1 jit_solution(11016323639982376423)
XLA Ops:
  0.6 69.6 %projection_backward.1 = (bf16[8,1024]{1,0:T(8,128)(2,1)S(1)}, bf16[1024,1024]{1,0:T(8,128)(2,1)S(1)}) custom-call(bf16[8,1024]{1,0:T(8,128)(2,1)} %h_hbm.1, bf16[1024,1024]{1,0:T(8,128)(2,1)} %w_hbm.1, s32[1,512]{1,0:T(1,128)} %bitcast.1, bf16[512]{0:T(512)(128)(2,1)} %up_hbm.1), custom_call_target="tpu_custom_call" | custom-call | flops 3221225472 | bytes 5242880 | tf_op jit(solution)/shard_map/projection_backward/pallas_call | solution.py:509
  70.2 0.6 copy.8
  70.8 1.3 %copy.9 = bf16[1024,1024]{1,0:T(8,128)(2,1)} copy(bf16[1024,1024]{1,0:T(8,128)(2,1)S(1)} %get-tuple-element.5) | data formatting | bytes 4194304
